TPU v7x, 512 devices: a whole 4x4x16 slice. The times are simulated.
512 devices in a mesh: cuts: 2 (over y_lo), dp: 16 (over z), row: 4 (over y_hi, core), col: 4 (over x).
Axes of the slice: x: 4, y: 4 (y_hi: 2, y_lo: 2; y = y_hi * 2 + y_lo), z: 16, core: 2. Of those that a mesh axis runs over, the one named last changes fastest.
Arguments:
- tokens: bfloat16 [32768, 4096], P(('cuts', 'dp'), 'row'), may hold values from -6 to 6
- cotangent: bfloat16 [32768, 4096], P(('cuts', 'dp'), 'col'), may hold values from -0.03125 to 0.03125
- norm_gain: float32 [4096], P('row'), may hold values from 0.5 to 6
- row_prev: float32 [4, 1024], P('row', 'dp'), may hold values from 0.02 to 0.5
- col_prev: float32 [4096], P('col'), may hold values from 0.002 to 0.05
Outputs:
- update: float32 [4, 1024, 4096], P('row', 'dp', 'col')
- row_moment: float32 [4, 1024], P('row', 'dp')
- col_moment: float32 [4096], P('col')
All inputs are finite; a program needn't handle non-finite values.
Results may differ from a plain program's by a relative error of at most 0.0004.
Values sent between devices are 32-bit elements; how exact they have to be, the bound alone decides.
A program may use at most 64 MiB of HBM per device.

v0:
```python
import jax
import jax.numpy as jnp
from jax import lax
from jax.sharding import PartitionSpec as P

D = 4096
F = 4096
decay_rate = 0.975
epsilon_one = 1e-30
clip_level = 1.0


def gradient_rows(inputs, cotangent, gains):
    product = lax.dot_general(
        inputs, cotangent, (((0,), (0,)), ((), ())), preferred_element_type=jnp.float32
    )
    return product * gains[:, None]


def adafactor_step(gradient, rows_prev, cols_prev, down_columns, all_total):
    squares = gradient * gradient
    row_sum = lax.psum(jnp.sum(squares, axis=1), "col")
    col_sum = down_columns(jnp.sum(squares, axis=0))
    row_moment = decay_rate * rows_prev + (1.0 - decay_rate) * (row_sum / F + epsilon_one)
    col_moment = decay_rate * cols_prev + (1.0 - decay_rate) * (col_sum / D + epsilon_one)
    factor = row_moment[:, None] * col_moment[None, :]
    raw_update = gradient / jnp.sqrt(factor)
    total_squares = all_total(jnp.sum(raw_update * raw_update))
    clip_scale = jnp.maximum(1.0, jnp.sqrt(total_squares / (D * F)) / clip_level)
    return (raw_update / clip_scale, row_moment, col_moment)


def body(tokens, cotangent, norm_gain, row_prev, col_prev):
    slice_part = lax.psum_scatter(
        gradient_rows(tokens, cotangent, norm_gain), "dp", scatter_dimension=0, tiled=True
    )
    gradient = lax.psum(slice_part, "cuts")
    update, row_moment, col_moment = adafactor_step(
        gradient,
        row_prev[0],
        col_prev,
        lambda values: lax.psum(values, ("dp", "row")),
        lambda values: lax.psum(values, ("dp", "row", "col")),
    )
    return (update[None], row_moment[None], col_moment)


def solution(mesh):
    return jax.shard_map(
        body,
        mesh=mesh,
        in_specs=(
            P(("cuts", "dp"), "row"),
            P(("cuts", "dp"), "col"),
            P("row"),
            P("row", "dp"),
            P("col"),
        ),
        out_specs=(P("row", "dp", "col"), P("row", "dp"), P("col")),
        check_vma=False,
    )
```

profile of v0, /device:TPU:2, one launch (start us, length us, event | category | flops | bytes accessed | tf_op | source)
XLA Modules:
  0.0 946.8 jit_solution(15512773143829418762)
XLA Ops:
  7.2 0.0 copy-start
  7.2 0.0 reduce-scatter.2.cloned.1.call-start
  7.2 1.5 copy-done
  8.8 5.9 convolution_multiply_fusion
  14.7 0.0 copy-start.4
  14.7 0.0 copy-start.2
  14.7 0.0 reduce-scatter.2.cloned.1.call-update
  14.7 0.0 all-reduce.2.cloned.1.call-start
  14.7 84.2 %reduce-scatter.2.cloned.1.call-done = f32[64,1024]{1,0:T(8,128)} async-done(((f32[1024,1024]{1,0:T(8,128)}), f32[64,1024]{1,0:T(8,128)}) %reduce-scatter.2.cloned.1.call-update) | async-done | bytes 262160 | tf_op jit(solution)/shard_map/reduce_scatter | solution.py:34
  99.0 0.0 all-reduce.2.cloned.1.call-update
  99.0 45.7 %all-reduce.2.cloned.1.call-done = f32[64,1024]{1,0:T(8,128)} async-done(((f32[64,1024]{1,0:T(8,128)}), f32[64,1024]{1,0:T(8,128)}) %all-reduce.2.cloned.1.call-update) | async-done | bytes 262160 | tf_op jit(solution)/shard_map/psum | solution.py:37
  144.7 1.1 multiply_reduce_fusion.2
  145.8 8.6 psum.29
  154.4 132.2 %psum.30 = f32[1024]{0:T(1024)S(1)} all-reduce(f32[1024]{0:T(1024)S(1)} %get-tuple-element.4), channel_id=1, replica_groups=mesh['cuts'=2,'dp'=16,'row'=4,'col'=4] {'dp','row'}, use_global_device_ids=true, to_apply=%region_5.0 | all-reduce | flops 1024 | bytes 8192 | tf_op jit(solution)/shard_map/psum | solution.py:42
  286.6 0.0 copy-done.4
  286.6 0.0 copy-done.2
  286.6 0.0 copy-start.3
  286.7 0.0 copy-start.1
  286.7 1.7 multiply_reduce_fusion
  288.4 649.1 %psum.31 = f32[]{:T(128)} all-reduce(f32[]{:T(128)} %multiply_reduce_fusion), channel_id=1, replica_groups=mesh['cuts'=2,'dp'=16,'row'=4,'col'=4] {'dp','row','col'}, use_global_device_ids=true, to_apply=%region_7.0 | all-reduce | flops 1 | bytes 8 | tf_op jit(solution)/shard_map/psum | solution.py:43
  938.2 1.8 divide_bitcast_fusion
  939.9 0.0 copy-done.3
  939.9 0.0 copy-done.1
  (2 shorter events, 0.0 us)
Async XLA Ops:
  7.2 1.6 copy-start
  7.2 91.8 %reduce-scatter.2.cloned.1.call-start = ((), (), s32[]{:S(2)}) async-start(), calls=%async_computation.1 | async-start | bytes 4456448 | tf_op jit(solution)/shard_map/reduce_scatter | solution.py:34
  14.7 272.0 %copy-start.4 = (f32[1,64]{1,0:T(1,128)S(1)}, f32[1,64]{1,0:T(1,128)}, u32[]{:S(2)}) copy-start(f32[1,64]{1,0:T(1,128)} %param.8) | copy-start | bytes 772
  14.7 272.0 %copy-start.2 = (f32[1024]{0:T(1024)S(1)}, f32[1024]{0:T(1024)}, u32[]{:S(2)}) copy-start(f32[1024]{0:T(1024)} %param.9) | copy-start | bytes 12292
  14.7 130.0 %all-reduce.2.cloned.1.call-start = ((), (), s32[]{:S(2)}) async-start(), calls=%async_computation.2 | async-start | bytes 524288 | tf_op jit(solution)/shard_map/psum | solution.py:37
  286.6 653.3 %copy-start.3 = (f32[64]{0:T(128)}, f32[64]{0:T(128)S(1)}, u32[]{:S(2)}) copy-start(f32[64]{0:T(128)S(1)} %bitcast_add_fusion) | copy-start | bytes 772
  286.7 653.3 %copy-start.1 = (f32[1024]{0:T(1024)}, f32[1024]{0:T(1024)S(1)}, u32[]{:S(2)}) copy-start(f32[1024]{0:T(1024)S(1)} %multiply_add_fusion) | copy-start | bytes 12292
Sparse Core Ops, SparseCore 0:
  14.8 84.1 reduce-scatter.1
  101.8 42.8 all-reduce.1
where the time goes:
time: 947 us
  blocking collectives  790 us (83%)
  waiting for transfers between devices  130 us (14%)
  between operations  14.8 us (2%)
    psum x1, blocking collectives, body(): lax.psum(values, ('dp', 'row', 'col'))  649 us
    psum x1, blocking collectives, body(): lax.psum(values, ('dp', 'row'))  132 us
    reduce_scatter x1, waiting for transfers between devices, body(): lax.psum_scatter(gradient_rows(tokens, cotangent, norm_gain), 'dp', scatt...  84.2 us
    psum x1, waiting for transfers between devices, body(): gradient = lax.psum(slice_part, 'cuts')  45.7 us
  transfers between devices with their start and end apart: 2, of which 2 were waited for; matrix products, arithmetic and copies ran while one was open for 0% of the time, Pallas kernels for 0%

commit v1 on v0

--- a/solution.py
+++ b/solution.py
@@ -39,7 +39,7 @@
         gradient,
         row_prev[0],
         col_prev,
-        lambda values: lax.psum(values, ("dp", "row")),
+        lambda values: lax.psum(lax.psum(values, "dp"), "row"),
         lambda values: lax.psum(values, ("dp", "row", "col")),
     )
     return (update[None], row_moment[None], col_moment)

time: 947 us -> 854 us (0.902)
  the two profiles are of different devices: /device:TPU:2 before, /device:TPU:8 now
where the time goes in v1:
time: 854 us; the launch traced here: 853 us
  blocking collectives  696 us (81%)
  waiting for transfers between devices  130 us (15%)
  between operations  14.8 us (2%)
    psum x1, blocking collectives, body(): lax.psum(values, ('dp', 'row', 'col'))  649 us
    reduce_scatter x1, waiting for transfers between devices, body(): lax.psum_scatter(gradient_rows(tokens, cotangent, norm_gain), 'dp', scatt...  84.3 us
    psum x1, waiting for transfers between devices, body(): gradient = lax.psum(slice_part, 'cuts')  45.6 us
    psum x1, blocking collectives, body(): lax.psum(values, 'dp')  31.3 us
  transfers between devices with their start and end apart: 2, of which 2 were waited for; matrix products, arithmetic and copies ran while one was open for 0% of the time, Pallas kernels for 0%

profile of v1, /device:TPU:8, one launch (start us, length us, event | category | flops | bytes accessed | tf_op | source)
XLA Modules:
  0.0 853.3 jit_solution(3671826420791679896)
XLA Ops:
  7.2 0.0 copy-start
  7.2 0.0 reduce-scatter.2.cloned.1.call-start
  7.2 1.5 copy-done
  8.8 5.9 convolution_multiply_fusion
  14.7 0.0 copy-start.4
  14.7 0.0 copy-start.2
  14.7 0.0 reduce-scatter.2.cloned.1.call-update
  14.7 0.0 all-reduce.2.cloned.1.call-start
  14.7 84.3 %reduce-scatter.2.cloned.1.call-done = f32[64,1024]{1,0:T(8,128)} async-done(((f32[1024,1024]{1,0:T(8,128)}), f32[64,1024]{1,0:T(8,128)}) %reduce-scatter.2.cloned.1.call-update) | async-done | bytes 262160 | tf_op jit(solution)/shard_map/reduce_scatter | solution.py:34
  99.0 0.0 all-reduce.2.cloned.1.call-update
  99.1 45.6 %all-reduce.2.cloned.1.call-done = f32[64,1024]{1,0:T(8,128)} async-done(((f32[64,1024]{1,0:T(8,128)}), f32[64,1024]{1,0:T(8,128)}) %all-reduce.2.cloned.1.call-update) | async-done | bytes 262160 | tf_op jit(solution)/shard_map/psum | solution.py:37
  144.7 1.1 multiply_reduce_fusion.2
  145.8 9.4 %psum.36 = f32[64]{0:T(128)S(1)} all-reduce(f32[64]{0:T(128)S(1)} %get-tuple-element.3), channel_id=1, replica_groups=mesh['cuts'=2,'dp'=16,'row'=4,'col'=4] {'col'}, use_global_device_ids=true, to_apply=%region_3.0 | all-reduce | flops 64 | bytes 512 | tf_op jit(solution)/shard_map/psum | solution.py:22
  155.2 31.3 %psum.37 = f32[1024]{0:T(1024)S(1)} all-reduce(f32[1024]{0:T(1024)S(1)} %get-tuple-element.4), channel_id=1, replica_groups=mesh['cuts'=2,'dp'=16,'row'=4,'col'=4] {'dp'}, use_global_device_ids=true, to_apply=%region_5.0 | all-reduce | flops 1024 | bytes 8192 | tf_op jit(solution)/shard_map/psum | solution.py:42
  186.5 7.2 psum.38
  193.7 0.0 copy-done.4
  193.7 0.0 copy-done.2
  193.7 0.0 copy-start.3
  193.7 0.0 copy-start.1
  193.7 1.7 multiply_reduce_fusion
  195.4 648.6 %psum.39 = f32[]{:T(128)} all-reduce(f32[]{:T(128)} %multiply_reduce_fusion), channel_id=1, replica_groups=mesh['cuts'=2,'dp'=16,'row'=4,'col'=4] {'dp','row','col'}, use_global_device_ids=true, to_apply=%region_8.0 | all-reduce | flops 1 | bytes 8 | tf_op jit(solution)/shard_map/psum | solution.py:43
  844.7 1.8 divide_bitcast_fusion
  846.5 0.0 copy-done.3
  846.5 0.0 copy-done.1
  (2 shorter events, 0.0 us)
Async XLA Ops:
  7.2 1.6 copy-start
  7.2 91.9 %reduce-scatter.2.cloned.1.call-start = ((), (), s32[]{:S(2)}) async-start(), calls=%async_computation.1 | async-start | bytes 4456448 | tf_op jit(solution)/shard_map/reduce_scatter | solution.py:34
  14.7 179.0 %copy-start.4 = (f32[1,64]{1,0:T(1,128)S(1)}, f32[1,64]{1,0:T(1,128)}, u32[]{:S(2)}) copy-start(f32[1,64]{1,0:T(1,128)} %param.8) | copy-start | bytes 772
  14.7 179.0 %copy-start.2 = (f32[1024]{0:T(1024)S(1)}, f32[1024]{0:T(1024)}, u32[]{:S(2)}) copy-start(f32[1024]{0:T(1024)} %param.9) | copy-start | bytes 12292
  14.7 130.0 %all-reduce.2.cloned.1.call-start = ((), (), s32[]{:S(2)}) async-start(), calls=%async_computation.2 | async-start | bytes 524288 | tf_op jit(solution)/shard_map/psum | solution.py:37
  193.7 652.8 %copy-start.3 = (f32[64]{0:T(128)}, f32[64]{0:T(128)S(1)}, u32[]{:S(2)}) copy-start(f32[64]{0:T(128)S(1)} %bitcast_add_fusion) | copy-start | bytes 772
  193.7 652.8 %copy-start.1 = (f32[1024]{0:T(1024)}, f32[1024]{0:T(1024)S(1)}, u32[]{:S(2)}) copy-start(f32[1024]{0:T(1024)S(1)} %multiply_add_fusion) | copy-start | bytes 12292
Sparse Core Ops, SparseCore 0:
  14.8 84.1 reduce-scatter.1
  101.9 42.7 all-reduce.1
